TPU v7x, 128 devices: a whole 4x4x4 slice. The times are simulated.
128 devices in a mesh: row: 16 (over y, x), col: 4 (over z), depth: 2 (over core).
Axes of the slice: x: 4, y: 4, z: 4, core: 2. Of those that a mesh axis runs over, the one named last changes fastest.
Arguments:
- upper: float32 [8192, 8192], P('row', 'col'), may hold values from -0.25 to 0.25
- pattern: int32 [64, 64], replicated, may hold values from 0 to 1, as said below
Outputs:
- purified: float32 [8192, 8192], P('row', 'col')
Inputs may be any that keep to these rules, and one draw needn't show every extreme that they name: `pattern`: block pairs near the diagonal are present; a few far pairs are present too.
All inputs are finite; a program needn't handle non-finite values.
Results may differ from a plain program's by a relative error of at most 0.00007.
Values sent between devices are 32-bit elements; how exact they have to be, the bound alone decides.
No kernel may reach another device: no remote copies, remote signals or barrier semaphores. Data moves between devices by JAX's collectives and lax.ppermute only.
A program may use at most 128 MiB of HBM per device.

v0:
```python
import jax
import jax.numpy as jnp
from jax import lax
from jax.sharding import PartitionSpec as P

BS = 128


def local(upper, pattern):
    rows_tile, cols_tile = upper.shape
    nrow = lax.axis_size("row")
    ncol = lax.axis_size("col")
    ndep = lax.axis_size("depth")
    row_blocks = rows_tile // BS
    col_blocks = cols_tile // BS
    spread = upper.reshape(row_blocks, ncol, BS // ncol, col_blocks, nrow, BS // nrow)
    spread = spread.transpose(4, 1, 0, 2, 3, 5).reshape(
        nrow * ncol, row_blocks, BS // ncol, col_blocks, BS // nrow
    )
    spread = lax.all_to_all(spread, ("row", "col"), split_axis=0, concat_axis=0, tiled=True)
    spread = spread.reshape(nrow, ncol, row_blocks, BS // ncol, col_blocks, BS // nrow)
    spread = spread.transpose(0, 2, 3, 1, 4, 5).reshape(
        ncol, col_blocks, BS // ncol, nrow, row_blocks, BS // nrow
    )
    spread = spread.transpose(3, 0, 4, 5, 1, 2).reshape(
        nrow * ncol, row_blocks, BS // nrow, col_blocks, BS // ncol
    )
    spread = lax.all_to_all(spread, ("row", "col"), split_axis=0, concat_axis=0, tiled=True)
    spread = spread.reshape(nrow, ncol, row_blocks, BS // nrow, col_blocks, BS // ncol)
    mirror = spread.transpose(2, 0, 3, 4, 1, 5).reshape(row_blocks, BS, col_blocks, BS)
    row_index = lax.axis_index("row")
    col_index = lax.axis_index("col")
    row_first = row_index * row_blocks
    col_first = col_index * col_blocks
    global_rows = row_first + jnp.arange(row_blocks, dtype=jnp.int32)
    global_cols = col_first + jnp.arange(col_blocks, dtype=jnp.int32)
    above = global_rows[:, None] < global_cols[None, :]
    below = global_rows[:, None] > global_cols[None, :]
    upper_pat = lax.dynamic_slice(pattern, (row_first, col_first), (row_blocks, col_blocks))
    lower_pat = lax.dynamic_slice(pattern, (col_first, row_first), (col_blocks, row_blocks)).T
    keep = jnp.where(above, upper_pat, jnp.where(below, lower_pat, 1)).astype(jnp.float32)
    own = upper.reshape(row_blocks, BS, col_blocks, BS)
    blended = jnp.where(
        above[:, None, :, None],
        own,
        jnp.where(below[:, None, :, None], mirror, 0.5 * (own + mirror)),
    )
    density = (blended * keep[:, None, :, None]).reshape(rows_tile, cols_tile)
    layer = lax.axis_index("depth")

    def layer_columns(tile):
        split = tile.reshape(rows_tile, col_blocks // ndep, ndep, BS)
        return lax.dynamic_slice_in_dim(split, layer, 1, 2).reshape(
            rows_tile, col_blocks // ndep * BS
        )

    split_rows = density.reshape(row_blocks // ndep, ndep, BS, cols_tile)
    layer_rows = lax.dynamic_slice_in_dim(split_rows, layer, 1, 1).reshape(
        row_blocks // ndep * BS, cols_tile
    )
    panel = lax.all_gather(layer_rows, "row", axis=0, tiled=True)

    def accumulate(piece):
        return jnp.dot(
            piece, panel, precision=lax.Precision.HIGHEST, preferred_element_type=jnp.float32
        )

    square_part = accumulate(lax.all_gather(layer_columns(density), "col", axis=1, tiled=True))
    square = lax.psum(square_part, "depth")
    cube_part = accumulate(lax.all_gather(layer_columns(square), "col", axis=1, tiled=True))
    cube = lax.psum(cube_part, "depth")
    return 3.0 * square - 2.0 * cube


def solution(mesh):
    placed = (P("row", "col"), P())
    return jax.shard_map(
        local, mesh=mesh, in_specs=placed, out_specs=P("row", "col"), check_vma=False
    )
```

profile of v0, /device:TPU:1, one launch (start us, length us, event | category | flops | bytes accessed | tf_op | source)
XLA Modules:
  0.0 894.1 jit_solution(12905529970818354647)
XLA Ops:
  11.9 13.3 %reshape.112 = f32[4,4,32,16,16,8]{2,1,0,5,4,3:T(4,128)} reshape(f32[512,2048]{0,1:T(8,128)} %copy.31) | data formatting | bytes 8388608 | tf_op jit(solution)/shard_map/reshape | solution.py:16
  25.2 15.8 %copy.33 = f32[16,4,4,32,16,8]{3,5,4,2,1,0:T(8,128)} copy(f32[16,4,4,32,16,8]{3,1,2,5,0,4:T(4,128)} %bitcast.47) | data formatting | bytes 8388608 | tf_op jit(solution)/shard_map/transpose | solution.py:17
  41.0 14.2 %reshape.132 = f32[64,1,16384]{2,1,0:T(1,128)} reshape(f32[64,4,16,8,32]{4,3,2,1,0:T(8,128)} %bitcast.44) | data formatting | bytes 8388608
  55.2 62.9 %all_to_all.10 = f32[64,1,16384]{2,1,0:T(1,128)} all-to-all(f32[64,1,16384]{2,1,0:T(1,128)} %reshape.132), channel_id=1, replica_groups=mesh['row'=16,'col'=4,'depth'=2] {'row','col'}, dimensions={0} | all-to-all | bytes 8388608 | tf_op jit(solution)/shard_map/all_to_all | solution.py:20
  118.6 13.7 %reduce.4 = f32[64,16384]{1,0:T(8,128)} reduce(f32[64,1,16384]{2,1,0:T(1,128)} %all_to_all.10, f32[]{:T(128)} %broadcast.66), dimensions={1}, to_apply=%all_to_all.6.reduce_sub_computation | reduce | bytes 8388612 | tf_op jit(solution)/shard_map/all_to_all | solution.py:20
  132.2 10.8 %reshape.133 = f32[64,4,16,8,32]{4,3,2,1,0:T(8,128)} reshape(f32[64,16384]{1,0:T(8,128)} %reduce.4) | data formatting | bytes 8388608
  149.5 15.3 %copy.35 = f32[16,4,4,8,16,32]{5,4,3,2,1,0:T(8,128)} copy(f32[16,4,4,8,16,32]{5,3,2,0,4,1:T(8,128)S(1)} %bitcast.48) | data formatting | bytes 8388608 | tf_op jit(solution)/shard_map/transpose | solution.py:25
  164.8 14.2 %reshape.134 = f32[64,1,16384]{2,1,0:T(1,128)} reshape(f32[64,4,8,16,32]{4,3,2,1,0:T(8,128)} %bitcast.46) | data formatting | bytes 8388608
  187.9 47.0 %all-to-all-done.1 = f32[64,1,16384]{2,1,0:T(1,128)} async-done(((f32[64,1,16384]{2,1,0:T(1,128)}), f32[64,1,16384]{2,1,0:T(1,128)}, u32[]{:S(2)}, u32[]{:S(2)}) %all-to-all-start.1) | async-done | bytes 4194336 | tf_op jit(solution)/shard_map/all_to_all | solution.py:28
  234.9 13.7 %reduce.5 = f32[64,16384]{1,0:T(8,128)} reduce(f32[64,1,16384]{2,1,0:T(1,128)} %all-to-all-done.1, f32[]{:T(128)} %broadcast.66), dimensions={1}, to_apply=%all_to_all.7.reduce_sub_computation | reduce | bytes 8388612 | tf_op jit(solution)/shard_map/all_to_all | solution.py:28
  248.6 10.8 %reshape.135 = f32[64,4,8,16,32]{4,3,2,1,0:T(8,128)} reshape(f32[64,16384]{1,0:T(8,128)} %reduce.5) | data formatting | bytes 8388608
  259.3 21.1 %copy.36 = f32[4,16,8,16,4,32]{5,4,2,1,0,3:T(4,128)} copy(f32[4,16,8,16,4,32]{5,3,2,0,4,1:T(8,128)} %bitcast.42) | data formatting | bytes 8388608 | tf_op jit(solution)/shard_map/transpose | solution.py:30
  280.4 13.5 %reshape.118 = f32[512,8,2,128]{3,0,2,1:T(8,128)} reshape(f32[4,16,8,16,4,32]{5,4,2,1,0,3:T(4,128)} %copy.36) | data formatting | bytes 8388608 | tf_op jit(solution)/shard_map/reshape | solution.py:30
  303.1 21.3 %copy.42 = f32[4,16,8,16,4,32]{5,4,3,2,1,0:T(4,128)} copy(f32[4,16,8,16,4,32]{5,3,2,0,4,1:T(8,128)} %bitcast.43) | data formatting | bytes 8388608 | tf_op jit(solution)/shard_map/transpose | solution.py:30
  324.4 18.4 %reshape.121 = f32[2,2,128,2048]{3,2,1,0:T(8,128)} reshape(f32[4,16,8,16,4,32]{5,4,3,2,1,0:T(4,128)} %copy.42) | data formatting | bytes 8388608 | tf_op jit(solution)/shard_map/reshape | solution.py:30
  347.0 42.5 %all-gather.4.cloned.1.call-done = f32[512,4096]{0,1:T(8,128)} async-done(((f32[512,1024]{0,1:T(8,128)}), f32[512,4096]{0,1:T(8,128)}) %all-gather.4.cloned.1.call-update) | async-done | bytes 8388624 | tf_op jit(solution)/shard_map/all_gather | solution.py:68
  389.5 199.9 %all-gather.6.cloned.1.call-done = f32[4096,2048]{1,0:T(8,128)} async-done(((f32[256,2048]{1,0:T(8,128)}), f32[4096,2048]{1,0:T(8,128)}) %all-gather.6.cloned.1.call-update) | async-done | bytes 33554448 | tf_op jit(solution)/shard_map/all_gather | solution.py:61
  589.5 60.8 %fusion.2 = f32[512,2048]{1,0:T(8,128)} fusion(f32[512,4096]{0,1:T(8,128)} %all-gather.4.cloned.1.call-done, f32[4096,2048]{1,0:T(8,128)} %all-gather.6.cloned.1.call-done), kind=kOutput, calls=%fused_computation.19 | convolution fusion | flops 51539607552 | bytes 46137344 | tf_op jit(solution)/shard_map/dot_general | solution.py:64
  650.4 34.3 %all-reduce.3.cloned.1.call-done = f32[512,2048]{1,0:T(8,128)} async-done(((f32[512,2048]{1,0:T(8,128)}), f32[512,2048]{1,0:T(8,128)}) %all-reduce.3.cloned.1.call-update) | async-done | bytes 4194320 | tf_op jit(solution)/shard_map/psum | solution.py:69
  691.2 8.2 dynamic-slice_reduce_fusion
  701.3 84.3 %all-gather.8.cloned.1.call-done = f32[512,4096]{1,0:T(8,128)} async-done(((f32[512,1024]{1,0:T(8,128)}), f32[512,4096]{1,0:T(8,128)}) %all-gather.8.cloned.1.call-update) | async-done | bytes 8388624 | tf_op jit(solution)/shard_map/all_gather | solution.py:70
  785.6 59.6 %fusion.3 = f32[512,2048]{1,0:T(8,128)} fusion(f32[512,4096]{1,0:T(8,128)} %all-gather.8.cloned.1.call-done, f32[4096,2048]{1,0:T(8,128)} %all-gather.6.cloned.1.call-done), kind=kOutput, calls=%fused_computation.20 | convolution fusion | flops 51539607552 | bytes 46137344 | tf_op jit(solution)/shard_map/dot_general | solution.py:64
  845.2 35.4 %all-reduce.5.cloned.1.call-done = f32[512,2048]{1,0:T(8,128)} async-done(((f32[512,2048]{1,0:T(8,128)}), f32[512,2048]{1,0:T(8,128)}) %all-reduce.5.cloned.1.call-update) | async-done | bytes 4194320 | tf_op jit(solution)/shard_map/psum | solution.py:71
  880.7 6.7 multiply_subtract_fusion
  (45 shorter events, 43.1 us)
Async XLA Ops:
  179.0 55.9 %all-to-all-start.1 = ((f32[64,1,16384]{2,1,0:T(1,128)}), f32[64,1,16384]{2,1,0:T(1,128)}, u32[]{:S(2)}, u32[]{:S(2)}) async-start(f32[64,1,16384]{2,1,0:T(1,128)} %reshape.134), calls=%async_computation.1 | async-start | bytes 8388608 | tf_op jit(solution)/shard_map/all_to_all | solution.py:28
  185.5 204.0 %all-gather.4.cloned.1.call-start = ((), (), s32[]{:S(2)}) async-start(), calls=%async_computation.2 | async-start | bytes 10485760 | tf_op jit(solution)/shard_map/all_gather | solution.py:68
  302.4 287.1 %all-gather.6.cloned.1.call-start = ((), (), s32[]{:S(2)}) async-start(), calls=%async_computation.3 | async-start | bytes 35651584 | tf_op jit(solution)/shard_map/all_gather | solution.py:61
  346.9 337.7 %all-reduce.3.cloned.1.call-start = ((), (), s32[]{:S(2)}) async-start(), calls=%async_computation.4 | async-start | bytes 8388608 | tf_op jit(solution)/shard_map/psum | solution.py:69
  650.3 135.3 %all-gather.8.cloned.1.call-start = ((), (), s32[]{:S(2)}) async-start(), calls=%async_computation.5 | async-start | bytes 10485760 | tf_op jit(solution)/shard_map/all_gather | solution.py:70
  701.2 179.4 %all-reduce.5.cloned.1.call-start = ((), (), s32[]{:S(2)}) async-start(), calls=%async_computation.6 | async-start | bytes 8388608 | tf_op jit(solution)/shard_map/psum | solution.py:71
Sparse Core Ops, SparseCore 0:
  302.5 86.9 all-gather.3
  391.6 197.7 all-gather.5
  650.4 34.1 all-reduce.2
  701.4 84.2 all-gather.7
  845.4 35.2 all-reduce.4
where the time goes:
time: 902 us; the launch traced here: 894 us
  waiting for transfers between devices  444 us (49%)
  local copies, waits for them, and re-layouts  204 us (23%)
  matrix products  120 us (13%)
  blocking collectives  62.9 us (7%)
  other arithmetic  42.5 us (5%)
  between operations  13.5 us (1%)
    all_gather x1, waiting for transfers between devices, local(): panel = lax.all_gather(layer_rows, 'row', axis=0, tiled=True)  200 us
    dot_general x2, matrix products, accumulate(): jnp.dot(piece, panel, precision=lax.Precision.HIGHEST, preferred_element_...  120 us
    all_gather x1, waiting for transfers between devices, local(): lax.all_gather(layer_columns(square), 'col', axis=1, tiled=True)  84.3 us
    all_to_all x1, blocking collectives, local(): lax.all_to_all(spread, ('row', 'col'), split_axis=0, concat_axis=0, tiled...  62.9 us
    unnamed x8, local copies, waits for them, and re-layouts  59 us
    all_to_all x1, waiting for transfers between devices, local(): lax.all_to_all(spread, ('row', 'col'), split_axis=0, concat_axis=0, tiled...  47 us
    all_gather x1, waiting for transfers between devices, local(): lax.all_gather(layer_columns(density), 'col', axis=1, tiled=True)  42.5 us
    transpose x2, local copies, waits for them, and re-layouts, local(): spread.transpose(2, 0, 3, 4, 1, 5).reshape(row_blocks, BS, col_blocks, BS)  42.4 us
  transfers between devices with their start and end apart: 6, of which 6 were waited for; matrix products, arithmetic and copies ran while one was open for 5% of the time, Pallas kernels for 0%

commit v1 on v0

--- a/solution.py
+++ b/solution.py
@@ -1,12 +1,254 @@
 import jax
 import jax.numpy as jnp
 from jax import lax
+from jax.experimental import pallas as pl
+from jax.experimental.pallas import tpu as pltpu
 from jax.sharding import PartitionSpec as P
 
 BS = 128
-
-
-def local(upper, pattern):
+NB = 64
+ROWS = 4
+COLS = 16
+NROW = 16
+NCOL = 4
+STRIPS = 16
+PER = 44
+CAP = 8 * PER
+SRC = 4
+HALF = 2
+MR = HALF * BS
+VMEM = 60 * 1024 * 1024
+ALL = ("row", "col", "depth")
+
+
+def prefix(ones):
+    ids = jnp.arange(NB, dtype=jnp.int32)
+    before = (ids[:, None] < ids[None, :]).astype(jnp.float32)
+    return jnp.dot(ones.astype(jnp.float32), before, preferred_element_type=jnp.float32).astype(jnp.int32)
+
+
+def layout(pattern):
+    ids = jnp.arange(NB, dtype=jnp.int32)
+    stored = jnp.where(ids[:, None] < ids[None, :], pattern, 0) + (ids[:, None] == ids[None, :])
+    stored = (stored != 0).astype(jnp.int32)
+    local = stored.reshape(NROW, ROWS, NCOL, COLS).transpose(0, 2, 1, 3).reshape(NB, NB)
+    rank = prefix(local)
+    count = jnp.sum(local, axis=1)
+    first = prefix(count[None, :])[0]
+    last = first + count
+    slot = (first[:, None] + rank).reshape(NROW, NCOL, ROWS, COLS).transpose(0, 2, 1, 3).reshape(NB, NB)
+    fits = jnp.all(((last - 1) >> 3) - (first >> 3) < SRC) & (last[NB - 1] <= CAP)
+    return stored, slot, local, rank, first, last, fits
+
+
+def pack_kernel(index_ref, upper_ref, out_ref):
+    shift = index_ref[16]
+
+    def one(e, _):
+        index = index_ref[e]
+
+        @pl.when(index >= 0)
+        def _():
+            a = index >> 4
+            b = index & 15
+            x = upper_ref[pl.ds(pl.multiple_of(a * BS, BS), BS), pl.ds(pl.multiple_of(b * BS, BS), BS)]
+
+            @pl.when(a + shift != b)
+            def _():
+                out_ref[:, e >> 2, e & 3] = x.reshape(STRIPS, 8, BS)
+
+            @pl.when(a + shift == b)
+            def _():
+                out_ref[:, e >> 2, e & 3] = (0.5 * (x + x.T)).reshape(STRIPS, 8, BS)
+
+        return 0
+
+    lax.fori_loop(0, 16, one, 0)
+
+
+def select_kernel(index_ref, got_ref, out_ref):
+    for u in range(PER):
+        out_ref[u] = got_ref[index_ref[u]]
+
+
+def split(x):
+    high = x.astype(jnp.bfloat16)
+    return high, (x - high.astype(jnp.float32)).astype(jnp.bfloat16)
+
+
+def main_kernel(sd_ref, st_ref, sn_ref, pd_ref, pt_ref, pn_ref, row_ref, rn_ref, where_ref, blocks_ref, out_ref,
+                a_ref, s_ref, acc_ref):
+    first_col = where_ref[0]
+    a_ref[...] = jnp.zeros_like(a_ref)
+    s_ref[NB] = jnp.zeros((2 * MR, BS), jnp.bfloat16)
+
+    def block(slot):
+        return blocks_ref[:, slot & 7, slot >> 3].reshape(BS, BS)
+
+    for h in range(HALF):
+        def fill(p, _, h=h):
+            code = row_ref[h, p]
+            m = code & 127
+            x = block((code >> 7) & 511)
+
+            def put(x):
+                high, low = split(x)
+                a_ref[m, h * BS:(h + 1) * BS] = high
+                a_ref[m, MR + h * BS:MR + (h + 1) * BS] = low
+
+            @pl.when(code < 65536)
+            def _():
+                put(x)
+
+            @pl.when(code >= 65536)
+            def _():
+                put(x.T)
+
+            return 0
+
+        lax.fori_loop(0, rn_ref[h], fill, 0)
+
+    def product(left_ref, d_ref, t_ref, k, p):
+        def operands(ref):
+            c0, c1 = ref[k, p], ref[k, p + 1]
+            left = jnp.concatenate([left_ref[c0 & 127], left_ref[c1 & 127]], axis=1)
+            return left, block(c0 >> 7), block(c1 >> 7)
+
+        left, x0, x1 = operands(d_ref)
+        h0, l0 = split(x0)
+        h1, l1 = split(x1)
+        right = jnp.concatenate([jnp.concatenate([h0, l0], axis=1), jnp.concatenate([h1, l1], axis=1)], axis=0)
+        z = jnp.dot(left, right, preferred_element_type=jnp.float32)
+        left, x0, x1 = operands(t_ref)
+        h0, l0 = split(x0)
+        h1, l1 = split(x1)
+        right = jnp.concatenate([jnp.concatenate([h0, h1], axis=1), jnp.concatenate([l0, l1], axis=1)], axis=0)
+        z += lax.dot_general(left, right, (((1,), (1,)), ((), ())), preferred_element_type=jnp.float32)
+        z = z[:MR] + z[MR:]
+        return z[:, :BS] + z[:, BS:]
+
+    def square(k, _):
+        acc_ref[...] = product(a_ref, sd_ref, st_ref, k, 0)
+
+        def step(i, _):
+            acc_ref[...] += product(a_ref, sd_ref, st_ref, k, 2 * i)
+            return 0
+
+        lax.fori_loop(1, sn_ref[k], step, 0)
+        x = acc_ref[...]
+        high, low = split(x)
+        s_ref[k, :MR] = high
+        s_ref[k, MR:] = low
+        j = k - first_col
+
+        @pl.when((j >= 0) & (j < COLS))
+        def _():
+            out_ref[:, pl.ds(pl.multiple_of(j * BS, BS), BS)] = 3.0 * x
+
+        return 0
+
+    lax.fori_loop(0, NB, square, 0)
+
+    def cube(j, _):
+        acc_ref[...] = product(s_ref, pd_ref, pt_ref, j, 0)
+
+        def step(i, _):
+            acc_ref[...] += product(s_ref, pd_ref, pt_ref, j, 2 * i)
+            return 0
+
+        lax.fori_loop(1, pn_ref[j], step, 0)
+        out_ref[:, pl.ds(pl.multiple_of(j * BS, BS), BS)] += -2.0 * acc_ref[...]
+        return 0
+
+    lax.fori_loop(0, COLS, cube, 0)
+
+
+def compact(chosen, codes, pad):
+    ids = jnp.arange(NB, dtype=jnp.int32)
+    at = jnp.where(chosen, prefix(chosen), -1)
+    hit = at[:, :, None] == ids[None, None, :]
+    return pad + jnp.sum(jnp.where(hit, (codes - pad)[:, :, None], 0), axis=1)
+
+
+def pairs(direct, mirrored):
+    most = jnp.maximum(jnp.sum(direct.astype(jnp.int32), axis=1), jnp.sum(mirrored.astype(jnp.int32), axis=1))
+    return (most + 1) >> 1
+
+
+SMEM = pl.BlockSpec(memory_space=pltpu.SMEM)
+INVMEM = pl.BlockSpec(memory_space=pltpu.VMEM)
+
+
+def sparse(upper, pattern):
+    ids = jnp.arange(NB, dtype=jnp.int32)
+    stored, slot, local, rank, first, last, _ = layout(pattern)
+    row, col, depth = lax.axis_index("row"), lax.axis_index("col"), lax.axis_index("depth")
+    chip = row * NCOL + col
+    mine = lax.dynamic_index_in_dim(local, chip, 0, False)
+    my_rank = lax.dynamic_index_in_dim(rank, chip, 0, False)
+    my_first = lax.dynamic_index_in_dim(first, chip, 0, False)
+    entry = jnp.arange(16, dtype=jnp.int32)
+    wanted = 8 * ((my_first >> 3) + (entry & 3)) + 2 * (entry >> 2) + depth - my_first
+    hit = (my_rank[None, :] == wanted[:, None]) & (mine[None, :] != 0)
+    index = jnp.sum(jnp.where(hit, ids[None, :] + 1, 0), axis=1) - 1
+    index = jnp.concatenate([index, (row * ROWS - col * COLS)[None]]).astype(jnp.int32)
+    packed = pl.pallas_call(
+        pack_kernel,
+        out_shape=jax.ShapeDtypeStruct((STRIPS, NCOL, SRC, 8, BS), jnp.float32),
+        in_specs=[SMEM, INVMEM],
+        out_specs=INVMEM,
+        compiler_params=pltpu.CompilerParams(vmem_limit_bytes=16 * 1024 * 1024),
+    )(index, upper)
+    got = lax.all_to_all(packed.reshape(NB, SRC * 8, BS), ("row", "col"), 0, 0, tiled=True)
+    u = jnp.arange(PER, dtype=jnp.int32)
+    g = 8 * u + 2 * col + depth
+    source = jnp.minimum(jnp.sum((last[None, :] <= g[:, None]).astype(jnp.int32), axis=1), NB - 1)
+    source_first = jnp.sum(jnp.where(source[:, None] == ids[None, :], first[None, :], 0), axis=1)
+    pick = source * SRC + jnp.clip(u - (source_first >> 3), 0, SRC - 1)
+    share = pl.pallas_call(
+        select_kernel,
+        out_shape=jax.ShapeDtypeStruct((PER, 8, BS), jnp.float32),
+        in_specs=[SMEM, INVMEM],
+        out_specs=INVMEM,
+        compiler_params=pltpu.CompilerParams(vmem_limit_bytes=16 * 1024 * 1024),
+    )(pick, got.reshape(NB * SRC, 8, BS))
+    blocks = lax.all_gather(share, ALL, axis=0).reshape(STRIPS, 8, PER, 8, BS)
+
+    below = ids[:, None] > ids[None, :]
+    both = jnp.where(below, stored.T, stored) != 0
+    slots = jnp.where(below, slot.T, slot)
+    codes = ids[None, :] + BS * slots
+    my_row = row * ROWS + depth * HALF
+    near = jnp.any(lax.dynamic_slice_in_dim(both, my_row, HALF, 0), axis=0)
+    direct = both & (ids[None, :] <= ids[:, None])
+    mirrored = both & (ids[None, :] > ids[:, None])
+    sd, st = direct & near[None, :], mirrored & near[None, :]
+    col_direct = lax.dynamic_slice_in_dim(direct, col * COLS, COLS, 0)
+    col_mirrored = lax.dynamic_slice_in_dim(mirrored, col * COLS, COLS, 0)
+    col_codes = lax.dynamic_slice_in_dim(codes, col * COLS, COLS, 0)
+    row_both = lax.dynamic_slice_in_dim(both, my_row, HALF, 0)
+    row_codes = lax.dynamic_slice_in_dim(codes + 65536 * below, my_row, HALF, 0)
+    half = pl.pallas_call(
+        main_kernel,
+        out_shape=jax.ShapeDtypeStruct((MR, COLS * BS), jnp.float32),
+        in_specs=[SMEM] * 9 + [INVMEM],
+        out_specs=INVMEM,
+        scratch_shapes=[
+            pltpu.VMEM((NB + 1, 2 * MR, BS), jnp.bfloat16),
+            pltpu.VMEM((NB + 1, 2 * MR, BS), jnp.bfloat16),
+            pltpu.VMEM((MR, BS), jnp.float32),
+        ],
+        compiler_params=pltpu.CompilerParams(vmem_limit_bytes=VMEM),
+    )(
+        compact(sd, codes, NB), compact(st, codes, NB), pairs(sd, st),
+        compact(col_direct, col_codes, NB), compact(col_mirrored, col_codes, NB), pairs(col_direct, col_mirrored),
+        compact(row_both, row_codes, NB), jnp.sum(row_both.astype(jnp.int32), axis=1),
+        (col * COLS)[None].astype(jnp.int32), blocks,
+    )
+    return lax.all_gather(half, "depth", axis=0, tiled=True)
+
+
+def dense(upper, pattern):
     rows_tile, cols_tile = upper.shape
     nrow = lax.axis_size("row")
     ncol = lax.axis_size("col")
@@ -72,6 +314,10 @@
     return 3.0 * square - 2.0 * cube
 
 
+def local(upper, pattern):
+    return lax.cond(layout(pattern)[-1], sparse, dense, upper, pattern)
+
+
 def solution(mesh):
     placed = (P("row", "col"), P())
     return jax.shard_map(

time: 902 us -> 224 us (0.25)
  waiting for transfers between devices: 444 us -> 114 us
  local copies, waits for them, and re-layouts: 204 us -> 7.02 us
  matrix products: 120 us -> 1.64 us
  blocking collectives: 62.9 us -> 0 us
  Pallas kernels: 0 us -> 60 us
  other arithmetic: 42.5 us -> 10.3 us
    all_gather x3 -> x2, waiting for transfers between devices: 327 us -> 97.2 us  [the longest x1 79.7 us: sparse(): blocks = lax.all_gather(share, ALL, axis=0).reshape(STRIPS, 8, PER, 8, BS)]
    dot_general x2 -> x8, matrix products: 120 us -> 1.64 us  [prefix(): jnp.dot(ones.astype(jnp.float32), before, preferred_element_type=jnp.floa...]
    transpose x4 -> x3, local copies, waits for them, and re-layouts: 73.5 us -> 0.19 us  [the longest x1 0.07 us: sparse(): both = jnp.where(below, stored.T, stored) != 0]
    psum x2 -> x0, waiting for transfers between devices: 69.7 us -> none  [the longest x1 35.4 us: local(): cube = lax.psum(cube_part, 'depth')]
    all_to_all x1 -> x0, blocking collectives: 62.9 us -> none  [local(): lax.all_to_all(spread, ('row', 'col'), split_axis=0, concat_axis=0, tiled...]
    pallas_call x0 -> x3, Pallas kernels: none -> 60 us  [the longest x1 55.3 us: sparse(): pl.pallas_call(main_kernel, out_shape=jax.ShapeDtypeStruct((MR, COLS * BS...]
    reshape x5 -> x6, local copies, waits for them, and re-layouts: 58.3 us -> 0.62 us  [the longest x3 0.35 us: layout(): stored.reshape(NROW, ROWS, NCOL, COLS).transpose(0, 2, 1, 3).reshape(NB, NB)]
    unnamed x8 -> x1, local copies, waits for them, and re-layouts: 59 us -> 4.7 us
  transfers between devices with their start and end apart: 6 -> 3, of which waited for: 6 -> 3; matrix products, arithmetic and copies ran while one was open for 5% -> 4% of each run, Pallas kernels for 0% -> 0%
where the time goes in v1:
time: 224 us; the launch traced here: 221 us
  waiting for transfers between devices  114 us (51%)
  Pallas kernels  60 us (27%)
  between operations  14.7 us (7%)
  starting transfers between devices  12.2 us (5%)
  other arithmetic  10.3 us (5%)
  local copies, waits for them, and re-layouts  7.02 us (3%)
    all_gather x1, waiting for transfers between devices, sparse(): blocks = lax.all_gather(share, ALL, axis=0).reshape(STRIPS, 8, PER, 8, BS)  79.7 us
    pallas_call x1, Pallas kernels, sparse(): pl.pallas_call(main_kernel, out_shape=jax.ShapeDtypeStruct((MR, COLS * BS...  55.3 us
    all_gather x1, waiting for transfers between devices, sparse(): return lax.all_gather(half, 'depth', axis=0, tiled=True)  17.5 us
    all_to_all x1, waiting for transfers between devices, sparse(): lax.all_to_all(packed.reshape(NB, SRC * 8, BS), ('row', 'col'), 0, 0, til...  17 us
    all_to_all x1, starting transfers between devices, sparse(): lax.all_to_all(packed.reshape(NB, SRC * 8, BS), ('row', 'col'), 0, 0, til...  12.1 us
    unnamed x1, local copies, waits for them, and re-layouts  4.7 us
  transfers between devices with their start and end apart: 3, of which 3 were waited for; matrix products, arithmetic and copies ran while one was open for 4% of the time, Pallas kernels for 0%

profile of v1, /device:TPU:1, one launch (start us, length us, event | category | flops | bytes accessed | tf_op | source)
XLA Modules:
  0.0 221.3 jit_solution(11873646334402993140)
XLA Ops:
  6.5 0.8 fusion.29
  7.4 0.3 reduce_sum.139
  7.9 0.8 compare_reduce_fusion
  8.6 0.7 slice.3
  10.7 199.1 %conditional.1 = (f32[512,2048]{1,0:T(8,128)}) conditional(s32[]{:T(128)} %convert_element_type.92, (f32[512,2048]{1,0:T(8,128)}, s32[64,64]{1,0:T(8,128)}) %tuple.11, (s32[64,64]{1,0:T(8,128)}, f32[512,2048]{1,0:T(8,128)}) %tuple.12), branch_computations={%region_2.5_spmd, %region_5.21_spmd} | conditional | flops 103089700864 | bytes 510151808 | solution.py:318
  10.9 0.8 fusion.7
  11.8 0.4 bitcast_reduce_fusion
  12.6 0.6 dynamic-slice.3
  14.0 0.6 add_subtract_fusion
  14.9 3.5 %branch_1_fun.3 = f32[16,4,4,8,128]{4,3,2,1,0:T(8,128)} custom-call(s32[17]{0:T(128)S(1)} %pad_add_fusion.index_ref, f32[512,2048]{1,0:T(8,128)} %get-tuple-element.19.upper_ref), custom_call_target="tpu_custom_call" | custom-call | tf_op jit(solution)/shard_map/cond/branch_1_fun/pallas_call | solution.py:195
  18.4 12.1 %all-to-all-start = ((f32[64,32,128]{2,1,0:T(8,128)}), f32[64,32,128]{2,1,0:T(8,128)S(1)}, u32[]{:S(2)}, u32[]{:S(2)}) async-start(f32[64,32,128]{2,1,0:T(8,128)} %bitcast.26), calls=%async_computation | async-start | bytes 2097152 | tf_op jit(solution)/shard_map/cond/branch_1_fun/all_to_all | solution.py:202
  31.0 17.0 %all-to-all-done = f32[64,32,128]{2,1,0:T(8,128)S(1)} async-done(((f32[64,32,128]{2,1,0:T(8,128)}), f32[64,32,128]{2,1,0:T(8,128)S(1)}, u32[]{:S(2)}, u32[]{:S(2)}) %all-to-all-start) | async-done | bytes 1048608 | tf_op jit(solution)/shard_map/cond/branch_1_fun/all_to_all | solution.py:202
  48.0 1.2 branch_1_fun.4
  50.7 0.6 select_reduce_fusion.2
  51.3 0.5 add_shift-right-arithmetic_fusion.1.sn_ref
  51.8 0.5 add_shift-right-arithmetic_fusion.pn_ref
  52.3 1.2 convert_reduce_fusion.5
  53.8 2.2 %select_reduce_fusion = (s32[64,64]{1,0:T(8,128)S(1)}, s32[64,64]{1,0:T(8,128)S(1)}) fusion(s32[64,64]{1,0:T(8,128)S(1)} %fusion, s32[64,64]{1,0:T(8,128)S(1)} %get-tuple-element.39, s32[64,64]{1,0:T(8,128)S(1)} %fusion.1), kind=kLoop, calls=%fused_computation | loop fusion | flops 1564672 | bytes 81920 | tf_op jit(solution)/shard_map/cond/branch_1_fun/reduce_sum | solution.py:170
  56.1 0.6 broadcast_add_fusion.4
  56.7 0.6 broadcast_add_fusion
  57.3 79.7 %all-gather.15.cloned.1.call-done = f32[5632,8,128]{2,1,0:T(8,128)} async-done(((f32[44,8,128]{2,1,0:T(8,128)}), f32[5632,8,128]{2,1,0:T(8,128)}) %all-gather.15.cloned.1.call-update) | async-done | bytes 23068688 | tf_op jit(solution)/shard_map/cond/branch_1_fun/all_gather | solution.py:215
  137.0 55.3 %branch_1_fun.5 = f32[256,2048]{1,0:T(8,128)} custom-call(s32[64,64]{1,0:T(8,128)} %get-tuple-element.53.sd_ref, s32[64,64]{1,0:T(8,128)} %get-tuple-element.52.st_ref, s32[64]{0:T(128)} %add_shift-right-arithmetic_fusion.1.sn_ref, s32[16,64]{1,0:T(8,128)} %get-tuple-element.57.pd_ref, s32[16,64]{1,0:T(8,128)} %get-tuple-element.56.pt_ref, ...), custom_call_target="tpu_custom_call" | custom-call | tf_op jit(solution)/shard_map/cond/branch_1_fun/pallas_call | solution.py:231
  192.3 17.5 %all-gather.13.cloned.1.call-done = f32[512,2048]{1,0:T(8,128)} async-done(((f32[256,2048]{1,0:T(8,128)}), f32[512,2048]{1,0:T(8,128)}) %all-gather.13.cloned.1.call-update) | async-done | bytes 4194320 | tf_op jit(solution)/shard_map/cond/branch_1_fun/all_gather | solution.py:248
  209.7 4.7 %copy.113 = f32[512,2048]{1,0:T(8,128)} copy(f32[512,2048]{1,0:T(8,128)} %get-tuple-element.20) | data formatting | bytes 8388608
  (45 shorter events, 3.2 us)
Async XLA Ops:
  14.9 34.9 %copy-start.1 = (s32[64,64]{1,0:T(8,128)S(1)}, s32[64,64]{1,0:T(8,128)}, u32[]{:S(2)}) copy-start(s32[64,64]{1,0:T(8,128)} %get-tuple-element.18) | copy-start | bytes 49156 | tf_op jit(solution)/shard_map/cond
  18.4 29.6 %all-to-all-start = ((f32[64,32,128]{2,1,0:T(8,128)}), f32[64,32,128]{2,1,0:T(8,128)S(1)}, u32[]{:S(2)}, u32[]{:S(2)}) async-start(f32[64,32,128]{2,1,0:T(8,128)} %bitcast.26), calls=%async_computation | async-start | bytes 2097152 | tf_op jit(solution)/shard_map/cond/branch_1_fun/all_to_all | solution.py:202
  30.5 106.4 %all-gather.15.cloned.1.call-start = ((), (), s32[]{:S(2)}) async-start(), calls=%async_computation.9 | async-start | bytes 23248896 | tf_op jit(solution)/shard_map/cond/branch_1_fun/all_gather | solution.py:215
  49.3 160.5 %all-gather.13.cloned.1.call-start = ((), (), s32[]{:S(2)}) async-start(), calls=%async_computation.8 | async-start | bytes 6291456 | tf_op jit(solution)/shard_map/cond/branch_1_fun/all_gather | solution.py:248
Sparse Core Ops, SparseCore 0:
  49.4 87.5 all-gather.14
  192.4 17.3 all-gather.12

commit v2 on v1

--- a/solution.py
+++ b/solution.py
@@ -17,7 +17,8 @@
 SRC = 4
 HALF = 2
 MR = HALF * BS
-VMEM = 60 * 1024 * 1024
+UNROLL = 8
+VMEM = 62 * 1024 * 1024
 ALL = ("row", "col", "depth")
 
 
@@ -76,14 +77,39 @@
     return high, (x - high.astype(jnp.float32)).astype(jnp.bfloat16)
 
 
-def main_kernel(sd_ref, st_ref, sn_ref, pd_ref, pt_ref, pn_ref, row_ref, rn_ref, where_ref, blocks_ref, out_ref,
-                a_ref, s_ref, acc_ref):
+def main_kernel(sd_ref, sdn_ref, st_ref, stn_ref, pd_ref, pdn_ref, pt_ref, ptn_ref, row_ref, rn_ref, where_ref,
+                blocks_hbm, out_ref, blocks_ref, a_ref, s_ref, sum_ref, cube_ref, item_ref, sem):
     first_col = where_ref[0]
+    loads = [
+        pltpu.make_async_copy(blocks_hbm.at[pl.ds(2 * i, 2)], blocks_ref.at[pl.ds(2 * i, 2)], sem.at[i])
+        for i in range(STRIPS // 2)
+    ]
+    for load in loads:
+        load.start()
     a_ref[...] = jnp.zeros_like(a_ref)
+    sum_ref[...] = jnp.zeros_like(sum_ref)
+    cube_ref[...] = jnp.zeros_like(cube_ref)
     s_ref[NB] = jnp.zeros((2 * MR, BS), jnp.bfloat16)
+
+    def list_items(count_ref, columns, at):
+        def column(k, n):
+            def one(i, n):
+                item_ref[at, n] = k * NB + 2 * i
+                return n + 1
+
+            return lax.fori_loop(0, (count_ref[k] + 1) >> 1, one, n)
+
+        n = lax.fori_loop(0, columns, column, 0)
+        for i in range(UNROLL - 1):
+            item_ref[at, n + i] = columns * NB
+        return (n + UNROLL - 1) // UNROLL
 
     def block(slot):
         return blocks_ref[:, slot & 7, slot >> 3].reshape(BS, BS)
+
+    rounds = [list_items(sdn_ref, NB, 0), list_items(stn_ref, NB, 1), list_items(pdn_ref, COLS, 2), list_items(ptn_ref, COLS, 3)]
+    for load in loads:
+        load.wait()
 
     for h in range(HALF):
         def fill(p, _, h=h):
@@ -108,80 +134,64 @@
 
         lax.fori_loop(0, rn_ref[h], fill, 0)
 
-    def product(left_ref, d_ref, t_ref, k, p):
-        def operands(ref):
-            c0, c1 = ref[k, p], ref[k, p + 1]
-            left = jnp.concatenate([left_ref[c0 & 127], left_ref[c1 & 127]], axis=1)
-            return left, block(c0 >> 7), block(c1 >> 7)
-
-        left, x0, x1 = operands(d_ref)
-        h0, l0 = split(x0)
-        h1, l1 = split(x1)
-        right = jnp.concatenate([jnp.concatenate([h0, l0], axis=1), jnp.concatenate([h1, l1], axis=1)], axis=0)
-        z = jnp.dot(left, right, preferred_element_type=jnp.float32)
-        left, x0, x1 = operands(t_ref)
-        h0, l0 = split(x0)
-        h1, l1 = split(x1)
-        right = jnp.concatenate([jnp.concatenate([h0, h1], axis=1), jnp.concatenate([l0, l1], axis=1)], axis=0)
-        z += lax.dot_general(left, right, (((1,), (1,)), ((), ())), preferred_element_type=jnp.float32)
+    def product(left_ref, list_ref, mirrored, k, p):
+        c0, c1 = list_ref[k, p], list_ref[k, p + 1]
+        left = jnp.concatenate([left_ref[c0 & 127], left_ref[c1 & 127]], axis=1)
+        h0, l0 = split(block(c0 >> 7))
+        h1, l1 = split(block(c1 >> 7))
+        if mirrored:
+            right = jnp.concatenate([jnp.concatenate([h0, h1], axis=1), jnp.concatenate([l0, l1], axis=1)], axis=0)
+            z = lax.dot_general(left, right, (((1,), (1,)), ((), ())), preferred_element_type=jnp.float32)
+        else:
+            right = jnp.concatenate([jnp.concatenate([h0, l0], axis=1), jnp.concatenate([h1, l1], axis=1)], axis=0)
+            z = jnp.dot(left, right, preferred_element_type=jnp.float32)
         z = z[:MR] + z[MR:]
         return z[:, :BS] + z[:, BS:]
 
-    def square(k, _):
-        acc_ref[...] = product(a_ref, sd_ref, st_ref, k, 0)
-
-        def step(i, _):
-            acc_ref[...] += product(a_ref, sd_ref, st_ref, k, 2 * i)
+    def work(left_ref, list_ref, mirrored, into_ref, at):
+        def several(i, _):
+            items = [item_ref[at, UNROLL * i + e] for e in range(UNROLL)]
+            done = [product(left_ref, list_ref, mirrored, item >> 6, item & 63) for item in items]
+            for item, z in zip(items, done):
+                into_ref[item >> 6] += z
             return 0
 
-        lax.fori_loop(1, sn_ref[k], step, 0)
-        x = acc_ref[...]
-        high, low = split(x)
+        lax.fori_loop(0, rounds[at], several, 0)
+
+    work(a_ref, sd_ref, False, sum_ref, 0)
+    work(a_ref, st_ref, True, sum_ref, 1)
+
+    def halves(k, _):
+        high, low = split(sum_ref[k])
         s_ref[k, :MR] = high
         s_ref[k, MR:] = low
-        j = k - first_col
-
-        @pl.when((j >= 0) & (j < COLS))
-        def _():
-            out_ref[:, pl.ds(pl.multiple_of(j * BS, BS), BS)] = 3.0 * x
-
         return 0
 
-    lax.fori_loop(0, NB, square, 0)
-
-    def cube(j, _):
-        acc_ref[...] = product(s_ref, pd_ref, pt_ref, j, 0)
-
-        def step(i, _):
-            acc_ref[...] += product(s_ref, pd_ref, pt_ref, j, 2 * i)
-            return 0
-
-        lax.fori_loop(1, pn_ref[j], step, 0)
-        out_ref[:, pl.ds(pl.multiple_of(j * BS, BS), BS)] += -2.0 * acc_ref[...]
-        return 0
-
-    lax.fori_loop(0, COLS, cube, 0)
+    lax.fori_loop(0, NB, halves, 0, unroll=2)
+    work(s_ref, pd_ref, False, cube_ref, 2)
+    work(s_ref, pt_ref, True, cube_ref, 3)
+    for j in range(COLS):
+        out_ref[:, j * BS:(j + 1) * BS] = 3.0 * sum_ref[first_col + j] - 2.0 * cube_ref[j]
 
 
 def compact(chosen, codes, pad):
     ids = jnp.arange(NB, dtype=jnp.int32)
     at = jnp.where(chosen, prefix(chosen), -1)
     hit = at[:, :, None] == ids[None, None, :]
-    return pad + jnp.sum(jnp.where(hit, (codes - pad)[:, :, None], 0), axis=1)
-
-
-def pairs(direct, mirrored):
-    most = jnp.maximum(jnp.sum(direct.astype(jnp.int32), axis=1), jnp.sum(mirrored.astype(jnp.int32), axis=1))
-    return (most + 1) >> 1
+    table = pad + jnp.sum(jnp.where(hit, (codes - pad)[:, :, None], 0), axis=1)
+    return jnp.pad(table, ((0, 1), (0, 0)), constant_values=pad)
+
+
+def count(chosen):
+    return jnp.sum(chosen.astype(jnp.int32), axis=1)
 
 
 SMEM = pl.BlockSpec(memory_space=pltpu.SMEM)
 INVMEM = pl.BlockSpec(memory_space=pltpu.VMEM)
 
 
-def sparse(upper, pattern):
-    ids = jnp.arange(NB, dtype=jnp.int32)
-    stored, slot, local, rank, first, last, _ = layout(pattern)
+def sparse(upper, pattern, stored, slot, local, rank, first, last):
+    ids = jnp.arange(NB, dtype=jnp.int32)
     row, col, depth = lax.axis_index("row"), lax.axis_index("col"), lax.axis_index("depth")
     chip = row * NCOL + col
     mine = lax.dynamic_index_in_dim(local, chip, 0, False)
@@ -214,6 +224,13 @@
     )(pick, got.reshape(NB * SRC, 8, BS))
     blocks = lax.all_gather(share, ALL, axis=0).reshape(STRIPS, 8, PER, 8, BS)
 
+    half = multiply(blocks, stored, slot)
+    return half, lax.ppermute(half, "depth", [(0, 1), (1, 0)])
+
+
+def multiply(blocks, stored, slot):
+    ids = jnp.arange(NB, dtype=jnp.int32)
+    row, col, depth = lax.axis_index("row"), lax.axis_index("col"), lax.axis_index("depth")
     below = ids[:, None] > ids[None, :]
     both = jnp.where(below, stored.T, stored) != 0
     slots = jnp.where(below, slot.T, slot)
@@ -228,24 +245,26 @@
     col_codes = lax.dynamic_slice_in_dim(codes, col * COLS, COLS, 0)
     row_both = lax.dynamic_slice_in_dim(both, my_row, HALF, 0)
     row_codes = lax.dynamic_slice_in_dim(codes + 65536 * below, my_row, HALF, 0)
-    half = pl.pallas_call(
+    return pl.pallas_call(
         main_kernel,
         out_shape=jax.ShapeDtypeStruct((MR, COLS * BS), jnp.float32),
-        in_specs=[SMEM] * 9 + [INVMEM],
+        in_specs=[SMEM] * 11 + [pl.BlockSpec(memory_space=pl.ANY)],
         out_specs=INVMEM,
         scratch_shapes=[
+            pltpu.VMEM((STRIPS, 8, PER, 8, BS), jnp.float32),
             pltpu.VMEM((NB + 1, 2 * MR, BS), jnp.bfloat16),
             pltpu.VMEM((NB + 1, 2 * MR, BS), jnp.bfloat16),
-            pltpu.VMEM((MR, BS), jnp.float32),
+            pltpu.VMEM((NB + 1, MR, BS), jnp.float32),
+            pltpu.VMEM((COLS + 1, MR, BS), jnp.float32),
+            pltpu.SMEM((4, NB * NB // 2 + NB + UNROLL), jnp.int32),
+            pltpu.SemaphoreType.DMA((STRIPS // 2,)),
         ],
         compiler_params=pltpu.CompilerParams(vmem_limit_bytes=VMEM),
     )(
-        compact(sd, codes, NB), compact(st, codes, NB), pairs(sd, st),
-        compact(col_direct, col_codes, NB), compact(col_mirrored, col_codes, NB), pairs(col_direct, col_mirrored),
-        compact(row_both, row_codes, NB), jnp.sum(row_both.astype(jnp.int32), axis=1),
-        (col * COLS)[None].astype(jnp.int32), blocks,
-    )
-    return lax.all_gather(half, "depth", axis=0, tiled=True)
+        compact(sd, codes, NB), count(sd), compact(st, codes, NB), count(st),
+        compact(col_direct, col_codes, NB), count(col_direct), compact(col_mirrored, col_codes, NB), count(col_mirrored),
+        compact(row_both, row_codes, NB), count(row_both), (col * COLS)[None].astype(jnp.int32), blocks,
+    )
 
 
 def dense(upper, pattern):
@@ -314,8 +333,17 @@
     return 3.0 * square - 2.0 * cube
 
 
+def dense_halves(upper, pattern, *tables):
+    whole = dense(upper, pattern)
+    depth = lax.axis_index("depth")
+    return tuple(lax.dynamic_slice_in_dim(whole, at * MR, MR, 0) for at in (depth, 1 - depth))
+
+
 def local(upper, pattern):
-    return lax.cond(layout(pattern)[-1], sparse, dense, upper, pattern)
+    *tables, fits = layout(pattern)
+    mine, other = lax.cond(fits, sparse, dense_halves, upper, pattern, *tables)
+    own = jnp.arange(2, dtype=jnp.int32) == lax.axis_index("depth")
+    return jnp.where(own[:, None, None], mine[None], other[None]).reshape(upper.shape)
 
 
 def solution(mesh):

time: 224 us -> 190 us (0.85)
  Pallas kernels: 60 us -> 37.8 us
  waiting for transfers between devices: 114 us -> 99.4 us
  other arithmetic: 10.3 us -> 14.4 us
    pallas_call x1, Pallas kernels: 55.3 us -> 33 us  [multiply(): pl.pallas_call(main_kernel, out_shape=jax.ShapeDtypeStruct((MR, COLS * BS...]
    all_gather x1 -> x0, waiting for transfers between devices: 17.5 us -> none  [sparse(): return lax.all_gather(half, 'depth', axis=0, tiled=True)]
    select_n x0 -> x1, other arithmetic: none -> 4.7 us  [local(): jnp.where(own[:, None, None], mine[None], other[None]).reshape(upper.shape)]
    ppermute x0 -> x1, waiting for transfers between devices: none -> 4.49 us  [sparse(): return (half, lax.ppermute(half, 'depth', [(0, 1), (1, 0)]))]
    unnamed x1 -> x4, local copies, waits for them, and re-layouts: 4.7 us -> 0.53 us
    pad x0 -> x5, local copies, waits for them, and re-layouts: none -> 3.03 us  [compact(): return jnp.pad(table, ((0, 1), (0, 0)), constant_values=pad)]
  transfers between devices with their start and end apart: 3 -> 3, of which waited for: 3 -> 3; matrix products, arithmetic and copies ran while one was open for 4% -> 5% of each run, Pallas kernels for 0% -> 0%
where the time goes in v2:
time: 190 us; the launch traced here: 187 us
  waiting for transfers between devices  99.4 us (52%)
  Pallas kernels  37.8 us (20%)
  between operations  14.8 us (8%)
  other arithmetic  14.4 us (8%)
  starting transfers between devices  12.2 us (6%)
  local copies, waits for them, and re-layouts  6.26 us (3%)
    all_gather x1, waiting for transfers between devices, sparse(): blocks = lax.all_gather(share, ALL, axis=0).reshape(STRIPS, 8, PER, 8, BS)  78.7 us
    pallas_call x1, Pallas kernels, multiply(): pl.pallas_call(main_kernel, out_shape=jax.ShapeDtypeStruct((MR, COLS * BS...  33 us
    all_to_all x1, waiting for transfers between devices, sparse(): lax.all_to_all(packed.reshape(NB, SRC * 8, BS), ('row', 'col'), 0, 0, til...  16.2 us
    all_to_all x1, starting transfers between devices, sparse(): lax.all_to_all(packed.reshape(NB, SRC * 8, BS), ('row', 'col'), 0, 0, til...  12 us
    select_n x1, other arithmetic, local(): jnp.where(own[:, None, None], mine[None], other[None]).reshape(upper.shape)  4.7 us
    ppermute x1, waiting for transfers between devices, sparse(): return (half, lax.ppermute(half, 'depth', [(0, 1), (1, 0)]))  4.49 us
  transfers between devices with their start and end apart: 3, of which 3 were waited for; matrix products, arithmetic and copies ran while one was open for 5% of the time, Pallas kernels for 0%

profile of v2, /device:TPU:1, one launch (start us, length us, event | category | flops | bytes accessed | tf_op | source)
XLA Modules:
  0.0 187.4 jit_solution(11750928446074153935)
XLA Ops:
  6.5 0.8 fusion.27
  7.4 1.2 fusion.28
  8.8 0.8 compare_reduce_fusion
  10.5 0.7 slice.3
  12.5 163.3 %conditional.1 = (f32[256,2048]{1,0:T(8,128)}, f32[256,2048]{1,0:T(8,128)}) conditional(s32[]{:T(128)} %convert_element_type.78, (f32[512,2048]{1,0:T(8,128)}, s32[64,64]{1,0:T(8,128)}) %tuple.13, (s32[64,64]{1,0:T(8,128)}, s32[16,4,4,16]{3,2,1,0:T(4,128)S(1)}, s32[64]{0:T(128)S(1)}, s32[64]{0:T(128)S(1)}, s32[64,64]{1,0:T(8,128)S(1)}, ...), branch_computations={%region_2.5_spmd, %region_5.20_spmd} | conditional | flops 103089700864 | bytes 518540416 | solution.py:344
  13.9 0.7 compare_bitcast_fusion
  15.2 0.7 add_subtract_fusion
  16.2 3.5 %branch_1_fun.3 = f32[16,4,4,8,128]{4,3,2,1,0:T(8,128)} custom-call(s32[17]{0:T(128)S(1)} %pad_add_fusion.index_ref, f32[512,2048]{1,0:T(8,128)} %get-tuple-element.34.upper_ref), custom_call_target="tpu_custom_call" | custom-call | tf_op jit(solution)/shard_map/cond/branch_1_fun/pallas_call | solution.py:205
  19.7 12.0 %all-to-all-start = ((f32[64,32,128]{2,1,0:T(8,128)}), f32[64,32,128]{2,1,0:T(8,128)S(1)}, u32[]{:S(2)}, u32[]{:S(2)}) async-start(f32[64,32,128]{2,1,0:T(8,128)} %bitcast.22), calls=%async_computation | async-start | bytes 2097152 | tf_op jit(solution)/shard_map/cond/branch_1_fun/all_to_all | solution.py:212
  32.0 0.8 select_reduce_fusion.5
  32.8 16.2 %all-to-all-done = f32[64,32,128]{2,1,0:T(8,128)S(1)} async-done(((f32[64,32,128]{2,1,0:T(8,128)}), f32[64,32,128]{2,1,0:T(8,128)S(1)}, u32[]{:S(2)}, u32[]{:S(2)}) %all-to-all-start) | async-done | bytes 1048608 | tf_op jit(solution)/shard_map/cond/branch_1_fun/all_to_all | solution.py:212
  49.0 1.2 branch_1_fun.4
  52.1 0.6 pad.16.pt_ref
  53.0 2.2 %select_reduce_fusion = (s32[64,64]{1,0:T(8,128)S(1)}, s32[64,64]{1,0:T(8,128)S(1)}) fusion(s32[64,64]{1,0:T(8,128)S(1)} %fusion, s32[64,64]{1,0:T(8,128)S(1)} %get-tuple-element.57, s32[64,64]{1,0:T(8,128)S(1)} %fusion.1), kind=kLoop, calls=%fused_computation | loop fusion | flops 1564672 | bytes 81920 | tf_op jit(solution)/shard_map/cond/branch_1_fun/reduce_sum | solution.py:181
  55.3 0.6 pad.13.sd_ref
  55.9 0.6 pad.14.st_ref
  56.8 0.6 pad.17.row_ref
  57.4 0.6 convert_reduce_fusion.5.rn_ref
  58.0 0.7 convert_reduce_fusion.3
  58.7 0.7 convert_reduce_fusion
  59.4 78.7 %all-gather.12.cloned.1.call-done = f32[5632,8,128]{2,1,0:T(8,128)} async-done(((f32[44,8,128]{2,1,0:T(8,128)}), f32[5632,8,128]{2,1,0:T(8,128)}) %all-gather.12.cloned.1.call-update) | async-done | bytes 23068688 | tf_op jit(solution)/shard_map/cond/branch_1_fun/all_gather | solution.py:225
  138.1 33.0 %branch_1_fun.5 = f32[256,2048]{1,0:T(8,128)} custom-call(s32[65,64]{1,0:T(8,128)} %pad.13.sd_ref, s32[64]{0:T(128)} %get-tuple-element.52.sdn_ref, s32[65,64]{1,0:T(8,128)} %pad.14.st_ref, s32[64]{0:T(128)} %get-tuple-element.51.stn_ref, s32[17,64]{1,0:T(8,128)} %pad.15.pd_ref, s32[16]{0:T(128)} %get-tuple-element.67.pdn_ref, s32[17,64]{1,0:T(8,128)} %pad.16.pt_ref, ...), custom_call_target="tpu_custom_call" | custom-call | tf_op jit(solution)/shard_map/cond/branch_1_fun/pallas_call | solution.py:248
  171.3 4.5 %collective-permute-done = f32[256,2048]{1,0:T(8,128)} collective-permute-done((f32[256,2048]{1,0:T(8,128)}, f32[256,2048]{1,0:T(8,128)}, u32[]{:S(2)}, u32[]{:S(2)}) %collective-permute-start) | collective-permute-done | bytes 2097184 | tf_op jit(solution)/shard_map/cond/branch_1_fun/ppermute | solution.py:228
  175.9 4.7 %bitcast_select_fusion.2 = f32[512,2048]{1,0:T(8,128)} fusion(f32[256,2048]{1,0:T(8,128)} %get-tuple-element.38, f32[256,2048]{1,0:T(8,128)} %get-tuple-element.37, pred[512]{0:T(512)(128)(4,1)S(1)} %broadcast_in_dim.222), kind=kLoop, calls=%fused_computation.92 | loop fusion | flops 1048576 | bytes 8389120 | tf_op jit(solution)/shard_map/jit(_where)/select_n | solution.py:346
  (56 shorter events, 5.3 us)
Async XLA Ops:
  7.3 2.2 %copy-start = (s32[64,64]{1,0:T(8,128)}, s32[64,64]{1,0:T(8,128)S(1)}, u32[]{:S(2)}) copy-start(s32[64,64]{1,0:T(8,128)S(1)} %fusion.27) | copy-start | bytes 49156
  9.7 0.6 copy-start.3
  12.7 0.6 copy-start.5
  12.7 6.9 %copy-start.4 = (s32[64]{0:T(128)}, s32[64]{0:T(128)S(1)}, u32[]{:S(2)}) copy-start(s32[64]{0:T(128)S(1)} %get-tuple-element.31) | copy-start | bytes 772 | tf_op jit(solution)/shard_map/cond
  13.3 18.5 %copy-start.6 = (s32[64]{0:T(128)S(1)}, s32[64]{0:T(128)}, u32[]{:S(2)}) copy-start(s32[64]{0:T(128)} %copy-done.5) | copy-start | bytes 772 | tf_op jit(solution)/shard_map/cond
  16.2 34.1 %copy-start.1 = (s32[64,64]{1,0:T(8,128)S(1)}, s32[64,64]{1,0:T(8,128)}, u32[]{:S(2)}) copy-start(s32[64,64]{1,0:T(8,128)} %get-tuple-element.28) | copy-start | bytes 49156 | tf_op jit(solution)/shard_map/cond
  19.7 29.3 %all-to-all-start = ((f32[64,32,128]{2,1,0:T(8,128)}), f32[64,32,128]{2,1,0:T(8,128)S(1)}, u32[]{:S(2)}, u32[]{:S(2)}) async-start(f32[64,32,128]{2,1,0:T(8,128)} %bitcast.22), calls=%async_computation | async-start | bytes 2097152 | tf_op jit(solution)/shard_map/cond/branch_1_fun/all_to_all | solution.py:212
  31.7 106.4 %all-gather.12.cloned.1.call-start = ((), (), s32[]{:S(2)}) async-start(), calls=%async_computation.8 | async-start | bytes 23248896 | tf_op jit(solution)/shard_map/cond/branch_1_fun/all_gather | solution.py:225
  171.2 4.6 %collective-permute-start = (f32[256,2048]{1,0:T(8,128)}, f32[256,2048]{1,0:T(8,128)}, u32[]{:S(2)}, u32[]{:S(2)}) collective-permute-start(f32[256,2048]{1,0:T(8,128)} %branch_1_fun.5), channel_id=1, source_target_pairs={{0,1},{1,0},{2,3},{3,2},{4,5},{5,4},{6,7},{7,6},{8,9},{9,8},{10,11... | collective-permute-start | bytes 6291464 | tf_op jit(solution)/shard_map/cond/branch_1_fun/ppermute | solution.py:228
Sparse Core Ops, SparseCore 0:
  50.4 87.6 all-gather.11

commit v3 on v2

--- a/solution.py
+++ b/solution.py
@@ -14,7 +14,7 @@
 STRIPS = 16
 PER = 44
 CAP = 8 * PER
-SRC = 4
+SRC = 3
 HALF = 2
 MR = HALF * BS
 UNROLL = 8
@@ -38,33 +38,59 @@
     first = prefix(count[None, :])[0]
     last = first + count
     slot = (first[:, None] + rank).reshape(NROW, NCOL, ROWS, COLS).transpose(0, 2, 1, 3).reshape(NB, NB)
-    fits = jnp.all(((last - 1) >> 3) - (first >> 3) < SRC) & (last[NB - 1] <= CAP)
-    return stored, slot, local, rank, first, last, fits
-
-
-def pack_kernel(index_ref, upper_ref, out_ref):
-    shift = index_ref[16]
-
-    def one(e, _):
-        index = index_ref[e]
-
-        @pl.when(index >= 0)
+    fits = jnp.all(count <= 8 * SRC) & (last[NB - 1] <= CAP)
+    return stored, slot, first, last, fits
+
+
+def pack_kernel(here_ref, pattern_ref, pattern_vec, upper_ref, out_ref, list_ref, sem):
+    row, col, depth = here_ref[0], here_ref[1], here_ref[2]
+    i = lax.broadcasted_iota(jnp.int32, (NB, NB), 0)
+    j = lax.broadcasted_iota(jnp.int32, (NB, NB), 1)
+    stored = (i == j) | ((i < j) & (pattern_vec[...] != 0))
+    earlier = (i // ROWS) * NCOL + j // COLS < row * NCOL + col
+    first = jnp.sum(jnp.where(stored & earlier, 1.0, 0.0)).astype(jnp.int32)
+
+    def copy(at):
+        code = list_ref[at]
+        a, b, n = code & 3, (code >> 2) & 15, code >> 6
+        return pltpu.make_async_copy(
+            upper_ref.at[pl.ds(a * STRIPS, STRIPS), :, pl.ds(pl.multiple_of(b * BS, BS), BS)],
+            out_ref.at[:, ((first + n) >> 1) & 3, n >> 3],
+            sem.at[at],
+        )
+
+    def find(a, state):
+        def one(b, state):
+            n, at = state
+            i, j = row * ROWS + a, col * COLS + b
+            there = (i == j) | ((i < j) & (pattern_ref[i, j] != 0))
+            ours = there & (((first + n) & 1) == depth) & (n < 8 * SRC)
+
+            @pl.when(ours)
+            def _():
+                list_ref[at] = a + 4 * b + 64 * n
+                copy(at).start()
+
+            return n + there.astype(jnp.int32), at + ours.astype(jnp.int32)
+
+        return lax.fori_loop(0, COLS, one, state)
+
+    _, found = lax.fori_loop(0, ROWS, find, (jnp.int32(0), jnp.int32(0)))
+
+    def finish(at, _):
+        copy(at).wait()
+        code = list_ref[at]
+        a, b, n = code & 3, (code >> 2) & 15, code >> 6
+
+        @pl.when(row * ROWS + a == col * COLS + b)
         def _():
-            a = index >> 4
-            b = index & 15
-            x = upper_ref[pl.ds(pl.multiple_of(a * BS, BS), BS), pl.ds(pl.multiple_of(b * BS, BS), BS)]
-
-            @pl.when(a + shift != b)
-            def _():
-                out_ref[:, e >> 2, e & 3] = x.reshape(STRIPS, 8, BS)
-
-            @pl.when(a + shift == b)
-            def _():
-                out_ref[:, e >> 2, e & 3] = (0.5 * (x + x.T)).reshape(STRIPS, 8, BS)
+            z = ((first + n) >> 1) & 3
+            x = out_ref[:, z, n >> 3].reshape(BS, BS)
+            out_ref[:, z, n >> 3] = (0.5 * (x + x.T)).reshape(STRIPS, 8, BS)
 
         return 0
 
-    lax.fori_loop(0, 16, one, 0)
+    lax.fori_loop(0, found, finish, 0)
 
 
 def select_kernel(index_ref, got_ref, out_ref):
@@ -188,33 +214,25 @@
 
 SMEM = pl.BlockSpec(memory_space=pltpu.SMEM)
 INVMEM = pl.BlockSpec(memory_space=pltpu.VMEM)
-
-
-def sparse(upper, pattern, stored, slot, local, rank, first, last):
+ANY = pl.BlockSpec(memory_space=pl.ANY)
+
+
+def gather(upper, pattern, first, last):
     ids = jnp.arange(NB, dtype=jnp.int32)
     row, col, depth = lax.axis_index("row"), lax.axis_index("col"), lax.axis_index("depth")
-    chip = row * NCOL + col
-    mine = lax.dynamic_index_in_dim(local, chip, 0, False)
-    my_rank = lax.dynamic_index_in_dim(rank, chip, 0, False)
-    my_first = lax.dynamic_index_in_dim(first, chip, 0, False)
-    entry = jnp.arange(16, dtype=jnp.int32)
-    wanted = 8 * ((my_first >> 3) + (entry & 3)) + 2 * (entry >> 2) + depth - my_first
-    hit = (my_rank[None, :] == wanted[:, None]) & (mine[None, :] != 0)
-    index = jnp.sum(jnp.where(hit, ids[None, :] + 1, 0), axis=1) - 1
-    index = jnp.concatenate([index, (row * ROWS - col * COLS)[None]]).astype(jnp.int32)
     packed = pl.pallas_call(
         pack_kernel,
         out_shape=jax.ShapeDtypeStruct((STRIPS, NCOL, SRC, 8, BS), jnp.float32),
-        in_specs=[SMEM, INVMEM],
+        in_specs=[SMEM, SMEM, INVMEM, ANY],
         out_specs=INVMEM,
+        scratch_shapes=[pltpu.SMEM((8 * SRC,), jnp.int32), pltpu.SemaphoreType.DMA((8 * SRC,))],
         compiler_params=pltpu.CompilerParams(vmem_limit_bytes=16 * 1024 * 1024),
-    )(index, upper)
+    )(jnp.stack([row, col, depth]).astype(jnp.int32), pattern, pattern, upper.reshape(ROWS * STRIPS, 8, COLS * BS))
     got = lax.all_to_all(packed.reshape(NB, SRC * 8, BS), ("row", "col"), 0, 0, tiled=True)
-    u = jnp.arange(PER, dtype=jnp.int32)
-    g = 8 * u + 2 * col + depth
+    g = 8 * jnp.arange(PER, dtype=jnp.int32) + 2 * col + depth
     source = jnp.minimum(jnp.sum((last[None, :] <= g[:, None]).astype(jnp.int32), axis=1), NB - 1)
     source_first = jnp.sum(jnp.where(source[:, None] == ids[None, :], first[None, :], 0), axis=1)
-    pick = source * SRC + jnp.clip(u - (source_first >> 3), 0, SRC - 1)
+    pick = source * SRC + jnp.clip((g - source_first) >> 3, 0, SRC - 1)
     share = pl.pallas_call(
         select_kernel,
         out_shape=jax.ShapeDtypeStruct((PER, 8, BS), jnp.float32),
@@ -222,13 +240,10 @@
         out_specs=INVMEM,
         compiler_params=pltpu.CompilerParams(vmem_limit_bytes=16 * 1024 * 1024),
     )(pick, got.reshape(NB * SRC, 8, BS))
-    blocks = lax.all_gather(share, ALL, axis=0).reshape(STRIPS, 8, PER, 8, BS)
-
-    half = multiply(blocks, stored, slot)
-    return half, lax.ppermute(half, "depth", [(0, 1), (1, 0)])
-
-
-def multiply(blocks, stored, slot):
+    return lax.all_gather(share, ALL, axis=0).reshape(STRIPS, 8, PER, 8, BS)
+
+
+def work_lists(stored, slot):
     ids = jnp.arange(NB, dtype=jnp.int32)
     row, col, depth = lax.axis_index("row"), lax.axis_index("col"), lax.axis_index("depth")
     below = ids[:, None] > ids[None, :]
@@ -245,10 +260,18 @@
     col_codes = lax.dynamic_slice_in_dim(codes, col * COLS, COLS, 0)
     row_both = lax.dynamic_slice_in_dim(both, my_row, HALF, 0)
     row_codes = lax.dynamic_slice_in_dim(codes + 65536 * below, my_row, HALF, 0)
+    return (
+        compact(sd, codes, NB), count(sd), compact(st, codes, NB), count(st),
+        compact(col_direct, col_codes, NB), count(col_direct), compact(col_mirrored, col_codes, NB), count(col_mirrored),
+        compact(row_both, row_codes, NB), count(row_both), (col * COLS)[None].astype(jnp.int32),
+    )
+
+
+def multiply(upper, pattern, blocks, *lists):
     return pl.pallas_call(
         main_kernel,
         out_shape=jax.ShapeDtypeStruct((MR, COLS * BS), jnp.float32),
-        in_specs=[SMEM] * 11 + [pl.BlockSpec(memory_space=pl.ANY)],
+        in_specs=[SMEM] * 11 + [ANY],
         out_specs=INVMEM,
         scratch_shapes=[
             pltpu.VMEM((STRIPS, 8, PER, 8, BS), jnp.float32),
@@ -260,11 +283,21 @@
             pltpu.SemaphoreType.DMA((STRIPS // 2,)),
         ],
         compiler_params=pltpu.CompilerParams(vmem_limit_bytes=VMEM),
-    )(
-        compact(sd, codes, NB), count(sd), compact(st, codes, NB), count(st),
-        compact(col_direct, col_codes, NB), count(col_direct), compact(col_mirrored, col_codes, NB), count(col_mirrored),
-        compact(row_both, row_codes, NB), count(row_both), (col * COLS)[None].astype(jnp.int32), blocks,
-    )
+    )(*lists, blocks)
+
+
+def join_kernel(depth_ref, mine_ref, other_ref, out_ref, sem):
+    depth = depth_ref[0]
+    copies = []
+    for k, (part_ref, half) in enumerate(((mine_ref, depth), (other_ref, 1 - depth))):
+        for i in range(4):
+            rows = MR // 4
+            to = pl.multiple_of(half * MR + i * rows, rows)
+            copies.append(pltpu.make_async_copy(part_ref.at[pl.ds(i * rows, rows)], out_ref.at[pl.ds(to, rows)], sem.at[k, i]))
+    for copy in copies:
+        copy.start()
+    for copy in copies:
+        copy.wait()
 
 
 def dense(upper, pattern):
@@ -333,17 +366,24 @@
     return 3.0 * square - 2.0 * cube
 
 
-def dense_halves(upper, pattern, *tables):
-    whole = dense(upper, pattern)
-    depth = lax.axis_index("depth")
-    return tuple(lax.dynamic_slice_in_dim(whole, at * MR, MR, 0) for at in (depth, 1 - depth))
+def dense_half(upper, pattern, *rest):
+    return lax.dynamic_slice_in_dim(dense(upper, pattern), lax.axis_index("depth") * MR, MR, 0)
 
 
 def local(upper, pattern):
-    *tables, fits = layout(pattern)
-    mine, other = lax.cond(fits, sparse, dense_halves, upper, pattern, *tables)
-    own = jnp.arange(2, dtype=jnp.int32) == lax.axis_index("depth")
-    return jnp.where(own[:, None, None], mine[None], other[None]).reshape(upper.shape)
+    stored, slot, first, last, fits = layout(pattern)
+    blocks = gather(upper, pattern, first, last)
+    lists = lax.optimization_barrier(work_lists(stored, slot))
+    mine = lax.cond(fits, multiply, dense_half, upper, pattern, blocks, *lists)
+    other = lax.ppermute(mine, "depth", [(0, 1), (1, 0)])
+    return pl.pallas_call(
+        join_kernel,
+        out_shape=jax.ShapeDtypeStruct(upper.shape, jnp.float32),
+        in_specs=[SMEM, ANY, ANY],
+        out_specs=ANY,
+        scratch_shapes=[pltpu.SemaphoreType.DMA((2, 4))],
+        compiler_params=pltpu.CompilerParams(vmem_limit_bytes=16 * 1024 * 1024),
+    )(lax.axis_index("depth")[None].astype(jnp.int32), mine, other)
 
 
 def solution(mesh):

time: 190 us -> 235 us (1.24)
  Pallas kernels: 37.8 us -> 98.7 us
  other arithmetic: 14.4 us -> 5.74 us
  local copies, waits for them, and re-layouts: 6.26 us -> 1.37 us
    pallas_call x2 -> x3, Pallas kernels: 4.75 us -> 70.8 us  [the longest x1 64.7 us: local(): pl.pallas_call(join_kernel, out_shape=jax.ShapeDtypeStruct(upper.shape, j...]
    pallas_call x1, Pallas kernels: 33 us -> 27.9 us  [multiply(): pl.pallas_call(main_kernel, out_shape=jax.ShapeDtypeStruct((MR, COLS * BS...]
    select_n x1 -> x0, other arithmetic: 4.7 us -> none  [local(): jnp.where(own[:, None, None], mine[None], other[None]).reshape(upper.shape)]
    all_to_all x1, waiting for transfers between devices: 16.2 us -> 12.4 us  [gather(): lax.all_to_all(packed.reshape(NB, SRC * 8, BS), ('row', 'col'), 0, 0, til...]
    pad x5, local copies, waits for them, and re-layouts: 3.03 us -> 0.03 us  [compact(): return jnp.pad(table, ((0, 1), (0, 0)), constant_values=pad)]
  transfers between devices with their start and end apart: 3 -> 3, of which waited for: 3 -> 3; matrix products, arithmetic and copies ran while one was open for 5% -> 3% of each run, Pallas kernels for 0% -> 0%
where the time goes in v3:
time: 235 us; the launch traced here: 233 us
  Pallas kernels  98.7 us (42%)
  waiting for transfers between devices  97.2 us (41%)
  between operations  14.8 us (6%)
  starting transfers between devices  13.9 us (6%)
  other arithmetic  5.74 us (2%)
    all_gather x1, waiting for transfers between devices, gather(): return lax.all_gather(share, ALL, axis=0).reshape(STRIPS, 8, PER, 8, BS)  80.8 us
    pallas_call x1, Pallas kernels, local(): pl.pallas_call(join_kernel, out_shape=jax.ShapeDtypeStruct(upper.shape, j...  64.7 us
    pallas_call x1, Pallas kernels, multiply(): pl.pallas_call(main_kernel, out_shape=jax.ShapeDtypeStruct((MR, COLS * BS...  27.9 us
    all_to_all x1, waiting for transfers between devices, gather(): lax.all_to_all(packed.reshape(NB, SRC * 8, BS), ('row', 'col'), 0, 0, til...  12.4 us
    all_to_all x1, starting transfers between devices, gather(): lax.all_to_all(packed.reshape(NB, SRC * 8, BS), ('row', 'col'), 0, 0, til...  12 us
    pallas_call x1, Pallas kernels, gather(): pl.pallas_call(pack_kernel, out_shape=jax.ShapeDtypeStruct((STRIPS, NCOL,...  4.88 us
  transfers between devices with their start and end apart: 3, of which 3 were waited for; matrix products, arithmetic and copies ran while one was open for 3% of the time, Pallas kernels for 0%

profile of v3, /device:TPU:1, one launch (start us, length us, event | category | flops | bytes accessed | tf_op | source)
XLA Modules:
  0.0 232.6 jit_solution(16858873775216495676)
XLA Ops:
  6.6 4.9 %shard_map.28 = f32[16,4,3,8,128]{4,3,2,1,0:T(8,128)} custom-call(s32[3]{0:T(128)S(1)} %pad_add_fusion.here_ref, s32[64,64]{1,0:T(8,128)} %pattern_vec.1, s32[64,64]{1,0:T(8,128)} %pattern_vec.1, f32[64,8,2048]{2,1,0:T(8,128)} %bitcast.83), custom_call_target="tpu_custom_call" | custom-call | tf_op jit(solution)/shard_map/pallas_call | solution.py:223
  11.5 12.0 %all-to-all-start.2 = ((f32[64,24,128]{2,1,0:T(8,128)}), f32[64,24,128]{2,1,0:T(8,128)S(1)}, u32[]{:S(2)}, u32[]{:S(2)}) async-start(f32[64,24,128]{2,1,0:T(8,128)} %bitcast.24), calls=%async_computation.2 | async-start | bytes 1572864 | tf_op jit(solution)/shard_map/all_to_all | solution.py:231
  23.9 1.2 bitcast_reduce_fusion
  25.2 0.1 fusion.27
  25.3 0.2 convert_reduce_fusion.2
  25.5 0.2 select_reduce_fusion.5
  25.7 12.4 %all-to-all-done.2 = f32[64,24,128]{2,1,0:T(8,128)S(1)} async-done(((f32[64,24,128]{2,1,0:T(8,128)}), f32[64,24,128]{2,1,0:T(8,128)S(1)}, u32[]{:S(2)}, u32[]{:S(2)}) %all-to-all-start.2) | async-done | bytes 786464 | tf_op jit(solution)/shard_map/all_to_all | solution.py:231
  38.1 1.2 shard_map.29
  39.4 0.5 slice.3
  40.6 0.6 compare_reduce_fusion
  41.8 0.2 reshape.176
  42.3 0.1 fusion.8
  42.7 0.1 fusion.3
  42.9 0.1 fusion.5
  43.0 2.2 select_reduce_fusion
  45.3 0.1 fusion.7
  45.5 0.1 fusion.6
  45.6 0.6 select_reduce_fusion.2
  46.5 80.8 %all-gather.12.cloned.1.call-done = f32[5632,8,128]{2,1,0:T(8,128)} async-done(((f32[44,8,128]{2,1,0:T(8,128)}), f32[5632,8,128]{2,1,0:T(8,128)}) %all-gather.12.cloned.1.call-update) | async-done | bytes 23068688 | tf_op jit(solution)/shard_map/all_gather | solution.py:243
  127.3 27.9 %conditional.1 = (f32[256,2048]{1,0:T(8,128)}) conditional(s32[]{:T(128)} %convert_element_type.81, (f32[512,2048]{1,0:T(8,128)}, s32[64,64]{1,0:T(8,128)S(1)}) %tuple.50, (f32[128,44,8,128]{3,2,1,0:T(8,128)}, s32[65,64]{1,0:T(8,128)S(1)}, s32[64]{0:T(128)S(1)}, s32[65,64]{1,0:T(8,128)S(1)}, s32[64]{0:T(128)S(1)}, ...), branch_computations={%region_15.18_spmd, %region_18.19_spmd} | conditional | flops 103088128000 | bytes 503794816 | solution.py:377
  127.3 27.9 %branch_1_fun.1 = f32[256,2048]{1,0:T(8,128)} custom-call(s32[65,64]{1,0:T(8,128)S(1)} %get-tuple-element.39.sd_ref, s32[64]{0:T(128)S(1)} %get-tuple-element.40.sdn_ref, s32[65,64]{1,0:T(8,128)S(1)} %get-tuple-element.41.st_ref, s32[64]{0:T(128)S(1)} %get-tuple-element.42.stn_ref, s32[17,64]{1,0:T(8,128)S(1)} %get-tuple-element.43.pd_ref, ...), custom_call_target="tpu_custom_call" | custom-call | tf_op jit(solution)/shard_map/cond/branch_1_fun/pallas_call | solution.py:271
  155.2 1.8 collective-permute-start
  157.0 4.0 %collective-permute-done.other_ref = f32[256,2048]{1,0:T(8,128)S(1)} collective-permute-done((f32[256,2048]{1,0:T(8,128)}, f32[256,2048]{1,0:T(8,128)S(1)}, u32[]{:S(2)}, u32[]{:S(2)}) %collective-permute-start) | collective-permute-done | bytes 2097184 | tf_op jit(solution)/shard_map/ppermute | solution.py:378
  161.0 64.7 %shard_map.30 = f32[512,2048]{1,0:T(8,128)} custom-call(s32[1]{0:T(128)} %bitcast.16.depth_ref, f32[256,2048]{1,0:T(8,128)} %get-tuple-element.111.mine_ref, f32[256,2048]{1,0:T(8,128)S(1)} %collective-permute-done.other_ref), custom_call_target="tpu_custom_call" | custom-call | tf_op jit(solution)/shard_map/pallas_call | solution.py:379
  (36 shorter events, 1.5 us)
Async XLA Ops:
  6.5 17.1 %copy-start = (s32[64,64]{1,0:T(8,128)S(1)}, s32[64,64]{1,0:T(8,128)}, u32[]{:S(2)}) copy-start(s32[64,64]{1,0:T(8,128)} %pattern_vec.1) | copy-start | bytes 49156
  11.5 26.6 %all-to-all-start.2 = ((f32[64,24,128]{2,1,0:T(8,128)}), f32[64,24,128]{2,1,0:T(8,128)S(1)}, u32[]{:S(2)}, u32[]{:S(2)}) async-start(f32[64,24,128]{2,1,0:T(8,128)} %bitcast.24), calls=%async_computation.2 | async-start | bytes 1572864 | tf_op jit(solution)/shard_map/all_to_all | solution.py:231
  23.6 103.8 %all-gather.12.cloned.1.call-start = ((), (), s32[]{:S(2)}) async-start(), calls=%async_computation.8 | async-start | bytes 23248896 | tf_op jit(solution)/shard_map/all_gather | solution.py:243
  155.2 5.8 %collective-permute-start = (f32[256,2048]{1,0:T(8,128)}, f32[256,2048]{1,0:T(8,128)S(1)}, u32[]{:S(2)}, u32[]{:S(2)}) collective-permute-start(f32[256,2048]{1,0:T(8,128)} %get-tuple-element.111.mine_ref), channel_id=1, source_target_pairs={{0,1},{1,0},{2,3},{3,2},{4,5},{5,4},{6,7},{7,6},{8,9},{9,8},{10,11... | collective-permute-start | bytes 6291464 | tf_op jit(solution)/shard_map/ppermute | solution.py:378
Sparse Core Ops, SparseCore 0:
  39.5 87.7 all-gather.11
